TPU v7x, 256 devices: a whole 4x4x8 slice. The times are simulated.
256 devices in a mesh: seq: 8 (over y_hi, x), mp: 32 (over y_lo, z, core).
Axes of the slice: x: 4, y: 4 (y_hi: 2, y_lo: 2; y = y_hi * 2 + y_lo), z: 8, core: 2. Of those that a mesh axis runs over, the one named last changes fastest.
Arguments:
- tokens: bfloat16 [768, 8192], P('mp', 'seq'), may hold values from -6 to 6
- gate_weight: bfloat16 [8192, 28672], P('seq', 'mp'), may hold values from -0.09375 to 0.09375
- up_weight: bfloat16 [8192, 28672], P('seq', 'mp'), may hold values from -0.09375 to 0.09375
- down_weight: bfloat16 [28672, 8192], P('mp', 'seq'), may hold values from -0.046875 to 0.046875
- gate_mask: int32 [64, 224], P('seq', 'mp'), may hold values 0 or 1
- up_mask: int32 [64, 224], P('seq', 'mp'), may hold values 0 or 1
- down_mask: int32 [224, 64], P('mp', 'seq'), may hold values 0 or 1
- grad_out: bfloat16 [768, 8192], P('mp', 'seq'), may hold values from -6 to 6
Outputs:
- mixed: bfloat16 [768, 8192], P('mp', 'seq')
- grad_tokens: bfloat16 [768, 8192], P('mp', 'seq')
- grad_gate: bfloat16 [8192, 28672], P('seq', 'mp')
- grad_up: bfloat16 [8192, 28672], P('seq', 'mp')
- grad_down: bfloat16 [28672, 8192], P('mp', 'seq')
All inputs are finite; a program needn't handle non-finite values. No bound on the sum of `gate_mask` or of `up_mask` or of `down_mask` on one device may be relied on, other than what follows from the above.
Results may differ from a plain program's by a relative error of at most 0.027.
Values may be sent and summed in bfloat16 or wider, within the bound.
A program may use at most 128 MiB of HBM per device.

v0:
```python
import math

import jax
import jax.numpy as jnp
from jax import lax
from jax.sharding import PartitionSpec as P


def apply_mask(weight, mask):
    block_rows, block_cols = mask.shape
    shaped = weight.reshape(
        block_rows, weight.shape[0] // block_rows, block_cols, weight.shape[1] // block_cols
    )
    return (shaped * mask.astype(weight.dtype)[:, None, :, None]).reshape(weight.shape)


def inner_left(left, right):
    return lax.dot_general(
        left, right, (((0,), (0,)), ((), ())), preferred_element_type=jnp.float32
    )


def inner_right(left, right):
    return lax.dot_general(
        left, right, (((1,), (1,)), ((), ())), preferred_element_type=jnp.float32
    )


def gate_forward(pre_gate, pre_up):
    sig_gate = jax.nn.sigmoid(pre_gate)
    silu_gate = pre_gate * sig_gate
    return (silu_gate * pre_up).astype(jnp.bfloat16)


def gate_backward(grad_hidden, pre_gate, pre_up):
    sig_gate = jax.nn.sigmoid(pre_gate)
    silu_gate = pre_gate * sig_gate
    grad_pre_gate = (grad_hidden * pre_up * sig_gate * (1.0 + pre_gate * (1.0 - sig_gate))).astype(
        jnp.bfloat16
    )
    grad_pre_up = (grad_hidden * silu_gate).astype(jnp.bfloat16)
    return (grad_pre_gate, grad_pre_up)


def on_device(tokens, gate_weight, up_weight, down_weight, gate_mask, up_mask, down_mask, grad_out):
    w_gate = apply_mask(gate_weight, gate_mask)
    w_up = apply_mask(up_weight, up_mask)
    w_down = apply_mask(down_weight, down_mask)
    inputs_all = lax.all_gather(tokens, "mp", axis=0, tiled=True)
    grad_scale = 1.0 / math.sqrt(inputs_all.shape[0])
    part_gate = jnp.dot(inputs_all, w_gate, preferred_element_type=jnp.float32)
    part_up = jnp.dot(inputs_all, w_up, preferred_element_type=jnp.float32)
    pre_gate, pre_up = (
        lax.psum(part_gate.astype(jnp.bfloat16), "seq").astype(jnp.float32),
        lax.psum(part_up.astype(jnp.bfloat16), "seq").astype(jnp.float32),
    )
    hidden = gate_forward(pre_gate, pre_up)
    mixed = lax.psum_scatter(
        jnp.dot(hidden, w_down, preferred_element_type=jnp.float32),
        "mp",
        scatter_dimension=0,
        tiled=True,
    ).astype(jnp.bfloat16)
    cotan_all = lax.all_gather(grad_out, "mp", axis=0, tiled=True)
    part_hidden = inner_right(cotan_all, w_down)
    grad_hidden = lax.psum(part_hidden.astype(jnp.bfloat16), "seq").astype(jnp.float32)
    grad_pre_gate, grad_pre_up = gate_backward(grad_hidden, pre_gate, pre_up)
    grad_down = apply_mask(inner_left(hidden, cotan_all) * grad_scale, down_mask).astype(
        jnp.bfloat16
    )
    grad_gate = apply_mask(inner_left(inputs_all, grad_pre_gate) * grad_scale, gate_mask).astype(
        jnp.bfloat16
    )
    grad_up = apply_mask(inner_left(inputs_all, grad_pre_up) * grad_scale, up_mask).astype(
        jnp.bfloat16
    )
    grad_tokens = lax.psum_scatter(
        inner_right(grad_pre_gate, w_gate) + inner_right(grad_pre_up, w_up),
        "mp",
        scatter_dimension=0,
        tiled=True,
    ).astype(jnp.bfloat16)
    return (mixed, grad_tokens, grad_gate, grad_up, grad_down)


def solution(mesh):
    placed = (
        P("mp", "seq"),
        P("seq", "mp"),
        P("seq", "mp"),
        P("mp", "seq"),
        P("seq", "mp"),
        P("seq", "mp"),
        P("mp", "seq"),
        P("mp", "seq"),
    )
    return jax.shard_map(
        on_device,
        mesh=mesh,
        in_specs=placed,
        out_specs=(P("mp", "seq"), P("mp", "seq"), P("seq", "mp"), P("seq", "mp"), P("mp", "seq")),
        check_vma=False,
    )
```

profile of v0, /device:TPU:1, one launch (start us, length us, event | category | flops | bytes accessed | tf_op | source)
XLA Modules:
  0.0 516.5 jit_solution(7250199610456082818)
XLA Ops:
  7.2 0.7 all-gather.3.cloned.1.call-update
  7.9 0.7 all-gather.5.cloned.1.call-update
  8.6 0.0 all-reduce.3.cloned.1.call-start
  8.7 0.8 fusion.25
  9.5 0.1 copy.17
  9.6 0.8 fusion.24
  10.3 0.1 copy.19
  10.4 3.9 copy.18
  14.3 2.4 copy.20
  16.7 61.7 %all-gather.3.cloned.1.call-done = bf16[768,1024]{1,0:T(8,128)(2,1)} async-done(((bf16[24,1024]{1,0:T(8,128)(2,1)}), bf16[768,1024]{1,0:T(8,128)(2,1)}) %all-gather.3.cloned.1.call-update) | async-done | bytes 1572880 | tf_op jit(solution)/shard_map/all_gather | solution.py:49
  78.4 0.3 mul.104
  78.8 4.8 fusion.12
  83.6 0.3 mul.108
  83.9 1.2 copy-done.6
  85.2 0.5 copy-done.1
  85.6 2.8 fusion.13
  88.4 55.9 %all-gather.5.cloned.1.call-done = bf16[768,1024]{1,0:T(8,128)(2,1)} async-done(((bf16[24,1024]{1,0:T(8,128)(2,1)}), bf16[768,1024]{1,0:T(8,128)(2,1)}) %all-gather.5.cloned.1.call-update) | async-done | bytes 1572880 | tf_op jit(solution)/shard_map/all_gather | solution.py:64
  144.3 0.3 mul.112
  144.6 1.2 copy-done.3
  145.8 0.5 copy-done.9
  146.3 4.2 fusion.14
  150.5 0.0 reduce-scatter.5.cloned.1.call-start
  150.5 113.9 %all-reduce.3.cloned.1.call-done = (bf16[768,896]{0,1:T(8,128)(2,1)}, bf16[768,896]{0,1:T(8,128)(2,1)}, bf16[768,896]{0,1:T(8,128)(2,1)}) async-done(((bf16[768,896]{0,1:T(8,128)(2,1)}, bf16[768,896]{0,1:T(8,128)(2,1)}, bf16[768,896]{0,1:T(8,128)(2,1)}), (bf16[768,896]{0,1:T(8,128)(2,1)}, bf16[768,896]{0,1:T(8,128)(2,1)}, bf16[768,896]{0,1:T(8,128)(2,1)})) %all-reduce.3.cloned.1.call-update) | async-done | bytes 4128784 | tf_op jit(solution)/shard_map/psum | solution.py:55
  264.4 6.0 %fusion.15 = f32[768,1024]{1,0:T(8,128)S(1)} fusion(bf16[1024,896]{0,1:T(8,128)(2,1)} %copy.18, bf16[112,8,8,128]{3,2,1,0:T(8,128)(2,1)} %bitcast.66, bf16[768,896]{0,1:T(8,128)(2,1)} %get-tuple-element.15, bf16[768,896]{0,1:T(8,128)(2,1)} %get-tuple-element.17, bf16[768,896]{0,1:T(8,128)(2,1)} %get-tuple-element.16), kind=kOutput, calls=%fused_computation.31 | convolution fusion | flops 1419149312 | bytes 10944512 | tf_op jit(solution)/shard_map/dot_general | solution.py:24
  270.5 3.8 convolution_add_fusion
  274.3 0.2 reduce-scatter.3.cloned.1.call-start
  274.5 1.2 copy-done.4
  275.8 6.1 %fusion.16 = f32[768,1024]{1,0:T(8,128)} fusion(bf16[896,1024]{1,0:T(8,128)(2,1)} %param.11, bf16[112,8,8,128]{3,2,1,0:T(8,128)(2,1)S(1)} %bitcast.64, bf16[768,896]{0,1:T(8,128)(2,1)} %get-tuple-element.15, bf16[768,896]{0,1:T(8,128)(2,1)} %get-tuple-element.16), kind=kOutput, calls=%fused_computation.32 | convolution fusion | flops 1415708672 | bytes 9568256 | tf_op jit(solution)/shard_map/dot_general | solution.py:59
  281.9 0.1 copy.21
  281.9 0.1 copy.22
  282.0 0.3 mul.127
  282.3 1.0 copy-done.15
  283.4 0.4 copy-done.19
  283.8 2.2 fusion.1
  286.0 2.5 copy.24
  288.4 0.3 mul.122
  288.7 1.0 copy-done.12
  289.8 0.4 copy-done.16
  290.2 4.0 fusion.2
  294.2 2.5 copy.23
  296.7 0.3 mul.131
  297.0 1.1 copy-done.10
  298.1 0.4 copy-done.13
  298.5 3.4 fusion
  301.8 87.9 %reduce-scatter.5.cloned.1.call-done = f32[24,1024]{1,0:T(8,128)} async-done(((f32[768,1024]{1,0:T(8,128)}), f32[24,1024]{1,0:T(8,128)}) %reduce-scatter.5.cloned.1.call-update) | async-done | bytes 98320 | tf_op jit(solution)/shard_map/reduce_scatter | solution.py:77
  389.7 1.5 convert_element_type.85
  391.3 117.2 %reduce-scatter.3.cloned.1.call-done = f32[24,1024]{1,0:T(8,128)} async-done(((f32[768,1024]{1,0:T(8,128)}), f32[24,1024]{1,0:T(8,128)}) %reduce-scatter.3.cloned.1.call-update) | async-done | bytes 98320 | tf_op jit(solution)/shard_map/reduce_scatter | solution.py:58
  508.4 1.5 convert_element_type.79
  (35 shorter events, 0.2 us)
Async XLA Ops:
  7.2 71.3 %all-gather.3.cloned.1.call-start = ((), (), s32[]{:S(2)}) async-start(), calls=%async_computation.2 | async-start | bytes 1622016 | tf_op jit(solution)/shard_map/all_gather | solution.py:49
  7.9 136.4 %all-gather.5.cloned.1.call-start = ((), (), s32[]{:S(2)}) async-start(), calls=%async_computation.4 | async-start | bytes 1622016 | tf_op jit(solution)/shard_map/all_gather | solution.py:64
  8.6 255.8 %all-reduce.3.cloned.1.call-start = ((), (), s32[]{:S(2)}) async-start(), calls=%async_computation.6 | async-start | bytes 8257536 | tf_op jit(solution)/shard_map/psum | solution.py:55
  10.4 3.9 copy-start
  14.3 2.4 copy-start.8
  16.7 62.0 %copy-start.2 = (bf16[1024,896]{0,1:T(8,128)(2,1)S(1)}, bf16[1024,896]{0,1:T(8,128)(2,1)}, u32[]{:S(2)}) copy-start(bf16[1024,896]{0,1:T(8,128)(2,1)} %copy.18) | copy-start | bytes 5505028
  78.7 4.8 copy-start.5
  78.8 6.4 %copy-start.11 = (bf16[768,1024]{1,0:T(8,128)(2,1)S(1)}, bf16[768,1024]{1,0:T(8,128)(2,1)}, u32[]{:S(2)}) copy-start(bf16[768,1024]{1,0:T(8,128)(2,1)} %all-gather.3.cloned.1.call-done) | copy-start | bytes 4718596
  83.6 2.0 copy-start.1
  83.9 1.3 copy-start.6
  144.3 2.0 copy-start.9
  144.6 1.2 copy-start.3
  150.5 239.3 %reduce-scatter.5.cloned.1.call-start = ((), (), s32[]{:S(2)}) async-start(), calls=%async_computation.5 | async-start | bytes 3244032 | tf_op jit(solution)/shard_map/reduce_scatter | solution.py:77
  264.4 6.1 %copy-start.7 = (bf16[8,128,7,128]{1,0,3,2:T(8,128)(2,1)S(1)}, bf16[8,128,7,128]{1,0,3,2:T(8,128)(2,1)}, u32[]{:S(2)}) copy-start(bf16[8,128,7,128]{1,0,3,2:T(8,128)(2,1)} %copy-done.6) | copy-start | bytes 5505028
  264.4 6.1 %copy-start.14 = (bf16[768,896]{0,1:T(8,128)(2,1)S(1)}, bf16[768,896]{0,1:T(8,128)(2,1)}, u32[]{:S(2)}) copy-start(bf16[768,896]{0,1:T(8,128)(2,1)} %get-tuple-element.16) | copy-start | bytes 4128772
  264.4 6.1 %copy-start.18 = (bf16[768,896]{0,1:T(8,128)(2,1)S(1)}, bf16[768,896]{0,1:T(8,128)(2,1)}, u32[]{:S(2)}) copy-start(bf16[768,896]{0,1:T(8,128)(2,1)} %get-tuple-element.17) | copy-start | bytes 4128772
  274.3 1.5 copy-start.4
  274.3 234.1 %reduce-scatter.3.cloned.1.call-start = ((), (), s32[]{:S(2)}) async-start(), calls=%async_computation.3 | async-start | bytes 3244032 | tf_op jit(solution)/shard_map/reduce_scatter | solution.py:58
  282.0 1.3 copy-start.15
  282.0 1.8 copy-start.19
  288.4 1.3 copy-start.12
  288.4 1.8 copy-start.16
  294.2 2.8 copy-start.17
  296.7 1.4 copy-start.10
  296.7 1.8 copy-start.13
Sparse Core Ops, SparseCore 0:
  9.9 68.5 all-gather.2
  80.3 63.9 all-gather.4
  150.6 113.7 all-reduce.2
  274.4 115.2 reduce-scatter.4
  392.1 116.2 reduce-scatter.2
where the time goes:
time: 520 us; the launch traced here: 516 us
  waiting for transfers between devices  438 us (84%)
  matrix products  37.1 us (7%)
  local copies, waits for them, and re-layouts  22.5 us (4%)
  between operations  14 us (3%)
    reduce_scatter x1, waiting for transfers between devices, on_device(): lax.psum_scatter(jnp.dot(hidden, w_down, preferred_element_type=jnp.float...  117 us
    psum x1, waiting for transfers between devices, on_device(): lax.psum(part_up.astype(jnp.bfloat16), 'seq').astype(jnp.float32)  114 us
    reduce_scatter x1, waiting for transfers between devices, on_device(): lax.psum_scatter(inner_right(grad_pre_gate, w_gate) + inner_right(grad_pr...  87.9 us
    all_gather x1, waiting for transfers between devices, on_device(): inputs_all = lax.all_gather(tokens, 'mp', axis=0, tiled=True)  61.7 us
    all_gather x1, waiting for transfers between devices, on_device(): cotan_all = lax.all_gather(grad_out, 'mp', axis=0, tiled=True)  55.9 us
    unnamed x44, local copies, waits for them, and re-layouts  20.3 us
    dot_general x3, matrix products, inner_right(): lax.dot_general(left, right, (((1,), (1,)), ((), ())), preferred_element_...  14 us
  transfers between devices with their start and end apart: 5, of which 5 were waited for; matrix products, arithmetic and copies ran while one was open for 8% of the time, Pallas kernels for 0%

commit v1 on v0

v1 whole, which is shorter than its diff:
```python
import functools
import math

import jax
import jax.numpy as jnp
from jax import lax
from jax.experimental import pallas as pl
from jax.experimental.pallas import tpu as pltpu
from jax.sharding import PartitionSpec as P

MESH = pl.DeviceIdType.MESH
BF = jnp.bfloat16
F32 = jnp.float32

TOK = 768
W = 1024
FH = 896
OWN = 24
CH = 48
R = 256
NCH = TOK // R
PR = R // 8
XR = R // 4
CA = 512
DZ = (1, 7, 2, 4, 3, 5, 6, 0)
NEG = tuple(DZ.index((8 - d) % 8) for d in DZ)
SELF = DZ.index(0)
NEED = [-(-(j + 1) * R // 96) for j in range(NCH)]
DONE = [0] + [((j + 1) * R) // 96 for j in range(NCH)]


def dot_nn(a, b):
    return jnp.dot(a, b, preferred_element_type=F32)


def dot_nt(a, b):
    return lax.dot_general(a, b, (((1,), (1,)), ((), ())), preferred_element_type=F32)


def dot_tn(a, b):
    return lax.dot_general(a, b, (((0,), (0,)), ((), ())), preferred_element_type=F32)


def loop(n, body):
    lax.fori_loop(0, n, lambda i, c: (body(i), c)[1], 0)


def kernel(
    tok_in, gw_in, uw_in, dw_in, gm, um, dm, cot_in,
    mix_out, gt_out, gg_out, gu_out, gd_out,
    wcat, wd, io_buf, slot_o, slot_s, tok, cot,
    p_gu, p_h, f1g, f1u, f2g, f2u, own_gu, sy_gu, fy_gu, fy_h, f1a, f1b, f2h,
    hid, gp, e_own, e_sib, e_sb, e_sr, ey_s, ey_r, ez_s, ez_r,
    lsem, ssem, rsem,
):
    s = lax.axis_index("seq")
    m = lax.axis_index("mp")
    h, x = s // 4, s % 4
    l, z, c = m // 16, (m // 2) % 8, m % 2
    xr, xl, xf = (x + 1) % 4, (x + 3) % 4, (x + 2) % 4
    oh = 1 - h

    def mp_of(dz, dl, dc=0):
        return ((l + dl) % 2) * 16 + ((z + dz) % 8) * 2 + (c + dc) % 2

    RIGHT, LEFT, YH = (h * 4 + xr, m), (h * 4 + xl, m), (oh * 4 + x, m)
    SIB, YL = (s, mp_of(0, 0, 1)), (s, mp_of(0, 1))

    def ZL(dz, dl):
        return (s, mp_of(dz, dl))

    ids, sent = {}, {}

    def send(key, src, dst, to):
        k = ids.setdefault(key, len(ids))
        d = pltpu.make_async_remote_copy(
            src_ref=src, dst_ref=dst, send_sem=ssem.at[k], recv_sem=rsem.at[k],
            device_id=to, device_id_type=MESH,
        )
        d.start()
        sent[key] = d

    def got(*keys):
        for key in keys:
            sent[key].wait_recv()

    loads = [
        pltpu.make_async_copy(tok_in, io_buf.at[0], lsem.at[0]),
        pltpu.make_async_copy(cot_in, io_buf.at[1], lsem.at[1]),
        pltpu.make_async_copy(gw_in, wcat.at[:, pl.ds(0, FH)], lsem.at[2]),
        pltpu.make_async_copy(uw_in, wcat.at[:, pl.ds(FH, FH)], lsem.at[3]),
        pltpu.make_async_copy(dw_in, wd, lsem.at[4]),
    ]
    for d in loads:
        d.start()

    barrier = pltpu.get_barrier_semaphore()
    peers = [RIGHT, LEFT, YH, SIB] + [
        ZL(dz, dl) for dz in range(8) for dl in range(2) if (dz, dl) != (0, 0)
    ]
    for to in peers:
        pl.semaphore_signal(barrier, inc=1, device_id=to, device_id_type=MESH)

    def pack(v):
        v = v.astype(F32)
        return jnp.concatenate([v[:, :512], v[:, 512:]], axis=0).astype(BF)

    def unpack(v):
        v = v.astype(F32)
        return jnp.concatenate([v[:OWN], v[OWN:]], axis=1)

    for a in range(2):
        loads[a].wait()
        slot_o[SELF, 0, a] = pack(io_buf[a])
    pl.semaphore_wait(barrier, len(peers))

    for q in range(8):
        p = NEG[q]
        for dl in range(2):
            if (DZ[p], dl) != (0, 0):
                send(("ag", q, dl), slot_o.at[SELF, 0], slot_o.at[q, dl], ZL(DZ[p], dl))

    def masked(w, ref, mask, rows, cols, col0):
        def body(i):
            r = pl.ds(pl.multiple_of(i * 128, 128), 128)
            for k in range(cols):
                cs = pl.ds(col0 + k * 128, 128)
                ref[r, cs] = (ref[r, cs].astype(F32) * mask[i, k].astype(F32)).astype(BF)
        loop(rows, body)

    loads[2].wait()
    masked(None, wcat, gm, 8, 7, 0)
    loads[3].wait()
    masked(None, wcat, um, 8, 7, FH)
    loads[4].wait()
    masked(None, wd, dm, 7, 8, 0)

    def share(q):
        for dl in range(2):
            if (DZ[q], dl) != (0, 0):
                got(("ag", q, dl))
        send(("sh", q), slot_o.at[q], slot_s.at[q], SIB)

    def assemble(q):
        got(("sh", q))
        for a, ref in ((0, tok), (1, cot)):
            for dl in range(2):
                v = jnp.concatenate([unpack(slot_o[q, dl, a]), unpack(slot_s[q, dl, a])], axis=0)
                ref[pl.ds(q * 96 + dl * CH, CH), :] = v.astype(BF)

    def rows_x(j, xi):
        return pl.ds(pl.multiple_of(j * R + xi * XR, XR), XR)

    def rows_p(j, xi, hi):
        return pl.ds(pl.multiple_of(j * R + xi * XR + hi * PR, PR), PR)

    G, U = pl.ds(0, FH), pl.ds(FH, FH)
    A, B = pl.ds(0, CA), pl.ds(CA, FH - CA)

    def part(j):
        rows = pl.ds(j * R, R)

        def body(n):
            cs = pl.ds(pl.multiple_of(n * 256, 256), 256)
            p_gu[rows, cs] = dot_nn(tok[rows, :], wcat[:, cs]).astype(BF)
        loop(7, body)
        send(("g1", j), p_gu.at[rows_x(j, xf), G], f1g.at[j], RIGHT)
        send(("u1", j), p_gu.at[rows_x(j, xf), U], f1u.at[j], LEFT)
        send(("g2l", j), p_gu.at[rows_x(j, xl), G], f2g.at[j, 1], LEFT)
        send(("u2r", j), p_gu.at[rows_x(j, xr), U], f2u.at[j, 0], RIGHT)

        def hbody(n):
            cs = pl.ds(pl.multiple_of(n * 256, 256), 256)
            v = dot_nt(cot[rows, :], wd[cs, :]).astype(BF)
            p_h[j, :, :, :, cs] = v.reshape(4, 2, PR, 256)
        loop(3, hbody)
        cs = pl.ds(768, 128)
        p_h[j, :, :, :, cs] = dot_nt(cot[rows, :], wd[cs, :]).astype(BF).reshape(4, 2, PR, 128)
        send(("hy", j), p_h.at[j, :, oh], fy_h.at[j], YH)

    def r1(j):
        got(("g1", j))
        rows = rows_x(j, xr)
        p_gu[rows, G] = (p_gu[rows, G].astype(F32) + f1g[j].astype(F32)).astype(BF)
        send(("g2r", j), p_gu.at[rows, G], f2g.at[j, 0], RIGHT)
        got(("u1", j))
        rows = rows_x(j, xl)
        p_gu[rows, U] = (p_gu[rows, U].astype(F32) + f1u[j].astype(F32)).astype(BF)
        send(("u2l", j), p_gu.at[rows, U], f2u.at[j, 1], LEFT)
        got(("hy", j))
        for xi in range(4):
            p_h[j, xi, h] = (p_h[j, xi, h].astype(F32) + fy_h[j, xi].astype(F32)).astype(BF)
        send(("h1a", j), p_h.at[j, xf, h, :, A], f1a.at[j], RIGHT)
        send(("h1b", j), p_h.at[j, xf, h, :, B], f1b.at[j], LEFT)
        send(("h2rb", j), p_h.at[j, xr, h, :, B], f2h.at[j, 0, :, B], RIGHT)
        send(("h2la", j), p_h.at[j, xl, h, :, A], f2h.at[j, 1, :, A], LEFT)

    def r2(j):
        got(("h1a", j))
        p_h[j, xr, h, :, A] = (p_h[j, xr, h, :, A].astype(F32) + f1a[j].astype(F32)).astype(BF)
        send(("h2ra", j), p_h.at[j, xr, h, :, A], f2h.at[j, 0, :, A], RIGHT)
        got(("h1b", j))
        p_h[j, xl, h, :, B] = (p_h[j, xl, h, :, B].astype(F32) + f1b[j].astype(F32)).astype(BF)
        send(("h2lb", j), p_h.at[j, xl, h, :, B], f2h.at[j, 1, :, B], LEFT)
        got(("g2l", j), ("u2r", j), ("g2r", j), ("u2l", j))
        for f2, cs in ((f2g, G), (f2u, U)):
            def total(hi):
                r = pl.ds(pl.multiple_of(hi * PR, PR), PR)
                return (
                    p_gu[rows_p(j, x, hi), cs].astype(F32)
                    + f2[j, 0, r, :].astype(F32)
                    + f2[j, 1, r, :].astype(F32)
                )
            sy_gu[j, :, cs] = total(oh).astype(BF)
            own_gu[j, :, cs] = total(h)
        send(("guy", j), sy_gu.at[j], fy_gu.at[j], YH)

    def r3(j):
        got(("guy", j), ("h2rb", j), ("h2la", j), ("h2ra", j), ("h2lb", j))
        mine = rows_p(j, x, h)
        step = 16

        def body(i):
            r = pl.ds(pl.multiple_of(i * step, step), step)
            pre_gate = own_gu[j, r, G] + fy_gu[j, r, G].astype(F32)
            pre_up = own_gu[j, r, U] + fy_gu[j, r, U].astype(F32)
            grad_hidden = (
                p_h[j, x, h, r, :].astype(F32) + f2h[j, 0, r, :].astype(F32) + f2h[j, 1, r, :].astype(F32)
            )
            sig = jax.nn.sigmoid(pre_gate)
            silu = pre_gate * sig
            rr = pl.ds(pl.multiple_of(j * R + x * XR + h * PR + i * step, step), step)
            hid[rr, :] = (silu * pre_up).astype(BF)
            gp[rr, G] = (grad_hidden * pre_up * sig * (1.0 + pre_gate * (1.0 - sig))).astype(BF)
            gp[rr, U] = (grad_hidden * silu).astype(BF)
        loop(PR // step, body)
        send(("py", j), gp.at[mine], gp.at[mine], YH)
        send(("pr0", j), gp.at[mine], gp.at[mine], RIGHT)
        send(("pl0", j), gp.at[mine], gp.at[mine], LEFT)
        send(("hr", j), hid.at[mine], hid.at[mine], RIGHT)
        send(("hl", j), hid.at[mine], hid.at[mine], LEFT)
        send(("hy0", j), hid.at[mine], hid.at[mine], YH)

    def a1(j):
        got(("py", j))
        other = rows_p(j, x, oh)
        send(("pr1", j), gp.at[other], gp.at[other], RIGHT)
        send(("pl1", j), gp.at[other], gp.at[other], LEFT)
        got(("pr0", j), ("pl0", j))
        fl, fr = rows_p(j, xl, h), rows_p(j, xr, h)
        send(("pfr0", j), gp.at[fl, G], gp.at[fl, G], RIGHT)
        send(("pfl0", j), gp.at[fr, U], gp.at[fr, U], LEFT)
        got(("hr", j), ("hl", j))
        send(("hfr", j), hid.at[fl, A], hid.at[fl, A], RIGHT)
        send(("hfl", j), hid.at[fr, B], hid.at[fr, B], LEFT)
        send(("hyl", j), hid.at[fl], hid.at[fl], YH)
        send(("hyr", j), hid.at[fr], hid.at[fr], YH)

    def a2(j):
        got(("pr1", j), ("pl1", j))
        fl, fr = rows_p(j, xl, oh), rows_p(j, xr, oh)
        send(("pfr1", j), gp.at[fl, G], gp.at[fl, G], RIGHT)
        send(("pfl1", j), gp.at[fr, U], gp.at[fr, U], LEFT)
        got(("hfr", j), ("hfl", j))
        ff = rows_p(j, xf, h)
        send(("hyf", j), hid.at[ff], hid.at[ff], YH)

    def d0(j):
        got(("pfr0", j), ("pfl0", j), ("pfr1", j), ("pfl1", j))
        got(("hy0", j), ("hyl", j), ("hyr", j), ("hyf", j))
        p0, p1 = DONE[j], DONE[j + 1]
        np_ = p1 - p0
        rows = pl.ds(p0 * 96, np_ * 96)

        def body(n):
            cs = pl.ds(pl.multiple_of(n * 256, 256), 256)
            er = pl.ds(pl.multiple_of((n // 2) * OWN, OWN), OWN)
            ec = pl.ds(pl.multiple_of((n % 2) * 256, 256), 256)
            for a in range(2):
                if a == 0:
                    v = dot_nn(hid[rows, :], wd[:, cs])
                else:
                    v = dot_nt(gp[rows, :], wcat[cs, :])
                v = v.reshape(np_, 2, 2, OWN, 256)
                for p in range(np_):
                    for dl in range(2):
                        e_own[a, dl, p0 + p, er, ec] = v[p, dl, 0]
                        e_sib[a, dl, p0 + p, er, ec] = v[p, dl, 1]
        loop(4, body)
        for dl in (1, 0):
            for a in range(2):
                for p in range(p0, p1):
                    e_sb[a, dl, p] = e_sib[a, dl, p].astype(BF)
                ps = pl.ds(p0, np_)
                send(("es", j, a, dl), e_sb.at[a, dl, ps], e_sr.at[a, dl, ps], SIB)

    def e2(j):
        p0, p1 = DONE[j], DONE[j + 1]
        ps = pl.ds(p0, p1 - p0)
        for a in range(2):
            got(("es", j, a, 1))
            for p in range(p0, p1):
                ey_s[a, p] = (e_own[a, 1, p] + e_sr[a, 1, p].astype(F32)).astype(BF)
            send(("ey", j, a), ey_s.at[a, ps], ey_r.at[a, ps], YL)

    def e3(j):
        p0, p1 = DONE[j], DONE[j + 1]
        for a in range(2):
            got(("es", j, a, 0), ("ey", j, a))
            for p in range(p0, p1):
                v = e_own[a, 0, p] + e_sr[a, 0, p].astype(F32) + ey_r[a, p].astype(F32)
                if DZ[p] == 0:
                    e_own[a, 0, p] = v
                else:
                    ez_s[a, p] = v.astype(BF)
                    send(("ez", p, a), ez_s.at[a, p], ez_r.at[a, p], ZL(DZ[p], 0))

    for q in range(NEED[0]):
        share(q)
    stages = [part, r1, r2, r3, a1, a2, d0, e2, e3]
    for t in range(NCH + len(stages) - 1):
        for k in reversed(range(len(stages))):
            j = t - k
            if 0 <= j < NCH:
                if k == 0:
                    if j + 1 < NCH:
                        for q in range(NEED[j], NEED[j + 1]):
                            share(q)
                    for q in range(NEED[j - 1] if j else 0, NEED[j]):
                        assemble(q)
                stages[k](j)

    scale = 1.0 / math.sqrt(TOK)

    def grads(i):
        cs = pl.ds(pl.multiple_of(i * 128, 128), 128)
        v = dot_tn(tok[:, cs], gp[...]) * scale
        for k in range(7):
            ks = pl.ds(k * 128, 128)
            gg_out[cs, ks] = (v[:, k * 128:(k + 1) * 128] * gm[i, k].astype(F32)).astype(BF)
            gu_out[cs, ks] = (v[:, FH + k * 128:FH + (k + 1) * 128] * um[i, k].astype(F32)).astype(BF)
    loop(8, grads)

    def gradd(i):
        cs = pl.ds(pl.multiple_of(i * 128, 128), 128)
        v = dot_tn(hid[:, cs], cot[...]) * scale
        for k in range(8):
            ks = pl.ds(k * 128, 128)
            gd_out[cs, ks] = (v[:, k * 128:(k + 1) * 128] * dm[i, k].astype(F32)).astype(BF)
    loop(7, gradd)

    for a, out in ((0, mix_out), (1, gt_out)):
        v = e_own[a, 0, SELF]
        for p in range(8):
            if p != SELF:
                got(("ez", p, a))
                v = v + ez_r[a, p].astype(F32)
        out[...] = jnp.concatenate([v[:OWN], v[OWN:]], axis=1).astype(BF)
    for d in sent.values():
        d.wait_send()


def on_device(tokens, gate_weight, up_weight, down_weight, gate_mask, up_mask, down_mask, grad_out):
    vm = pl.BlockSpec(memory_space=pltpu.VMEM)
    sm = pl.BlockSpec(memory_space=pltpu.SMEM)
    hbm = pl.BlockSpec(memory_space=pl.ANY)
    n_msg = 15 + 8 + NCH * (4 + 1 + 6 + 3 + 6 + 8 + 3 + 4 + 2) + 14
    V = pltpu.VMEM
    scratch = [
        V((W, 2 * FH), BF), V((FH, W), BF), V((2, OWN, W), BF),
        V((8, 2, 2, CH, 512), BF), V((8, 2, 2, CH, 512), BF), V((TOK, W), BF), V((TOK, W), BF),
        V((TOK, 2 * FH), BF), V((NCH, 4, 2, PR, FH), BF),
        V((NCH, XR, FH), BF), V((NCH, XR, FH), BF),
        V((NCH, 2, XR, FH), BF), V((NCH, 2, XR, FH), BF),
        V((NCH, PR, 2 * FH), F32), V((NCH, PR, 2 * FH), BF), V((NCH, PR, 2 * FH), BF),
        V((NCH, 4, PR, FH), BF), V((NCH, PR, CA), BF), V((NCH, PR, FH - CA), BF), V((NCH, 2, PR, FH), BF),
        V((TOK, FH), BF), V((TOK, 2 * FH), BF),
        V((2, 2, 8, CH, 512), F32), V((2, 2, 8, CH, 512), F32),
        V((2, 2, 8, CH, 512), BF), V((2, 2, 8, CH, 512), BF),
        V((2, 8, CH, 512), BF), V((2, 8, CH, 512), BF), V((2, 8, CH, 512), BF), V((2, 8, CH, 512), BF),
        pltpu.SemaphoreType.DMA((5,)), pltpu.SemaphoreType.DMA((n_msg,)), pltpu.SemaphoreType.DMA((n_msg,)),
    ]
    return pl.pallas_call(
        kernel,
        out_shape=(
            jax.ShapeDtypeStruct((OWN, W), BF),
            jax.ShapeDtypeStruct((OWN, W), BF),
            jax.ShapeDtypeStruct((W, FH), BF),
            jax.ShapeDtypeStruct((W, FH), BF),
            jax.ShapeDtypeStruct((FH, W), BF),
        ),
        in_specs=[hbm, hbm, hbm, hbm, sm, sm, sm, hbm],
        out_specs=(vm, vm, vm, vm, vm),
        scratch_shapes=scratch,
        name="layer",
        compiler_params=pltpu.CompilerParams(
            collective_id=0, has_side_effects=True, vmem_limit_bytes=60 << 20
        ),
        cost_estimate=pl.CostEstimate(flops=9 * 2 * TOK * W * FH, bytes_accessed=12 << 20, transcendentals=TOK * FH),
    )(tokens, gate_weight, up_weight, down_weight, gate_mask, up_mask, down_mask, grad_out)


def solution(mesh):
    placed = (
        P("mp", "seq"),
        P("seq", "mp"),
        P("seq", "mp"),
        P("mp", "seq"),
        P("seq", "mp"),
        P("seq", "mp"),
        P("mp", "seq"),
        P("mp", "seq"),
    )
    return jax.shard_map(
        on_device,
        mesh=mesh,
        in_specs=placed,
        out_specs=(P("mp", "seq"), P("mp", "seq"), P("seq", "mp"), P("seq", "mp"), P("mp", "seq")),
        check_vma=False,
    )
```

time: 520 us -> 146 us (0.28)
  waiting for transfers between devices: 438 us -> 0 us
  Pallas kernels: 0 us -> 134 us
  matrix products: 37.1 us -> 0 us
  between operations: 14 us -> 0.65 us
  local copies, waits for them, and re-layouts: 22.5 us -> 9.24 us
    reduce_scatter x2 -> x0, waiting for transfers between devices: 205 us -> none  [the longest x1 117 us: on_device(): lax.psum_scatter(jnp.dot(hidden, w_down, preferred_element_type=jnp.float...]
    pallas_call x0 -> x1, Pallas kernels: none -> 134 us  [on_device(): pl.pallas_call(kernel, out_shape=(jax.ShapeDtypeStruct((OWN, W), BF), jax...]
    all_gather x2 -> x0, waiting for transfers between devices: 118 us -> none  [the longest x1 61.7 us: on_device(): inputs_all = lax.all_gather(tokens, 'mp', axis=0, tiled=True)]
    psum x1 -> x0, waiting for transfers between devices: 114 us -> none  [on_device(): lax.psum(part_up.astype(jnp.bfloat16), 'seq').astype(jnp.float32)]
    dot_general x9 -> x0, matrix products: 37.1 us -> none  [the longest x3 14 us: inner_right(): lax.dot_general(left, right, (((1,), (1,)), ((), ())), preferred_element_...]
    unnamed x44 -> x9, local copies, waits for them, and re-layouts: 20.3 us -> 9.24 us
  transfers between devices with their start and end apart: 5 -> 0, of which waited for: 5 -> 0; matrix products, arithmetic and copies ran while one was open for 8% -> 0% of each run, Pallas kernels for 0% -> 0%
where the time goes in v1:
time: 146 us; the launch traced here: 144 us
  Pallas kernels  134 us (92%)
  local copies, waits for them, and re-layouts  9.24 us (6%)
    pallas_call x1, Pallas kernels, on_device(): pl.pallas_call(kernel, out_shape=(jax.ShapeDtypeStruct((OWN, W), BF), jax...  134 us
    unnamed x9, local copies, waits for them, and re-layouts  9.24 us

profile of v1, /device:TPU:1, one launch (start us, length us, event | category | flops | bytes accessed | tf_op | source)
XLA Modules:
  0.0 143.8 jit_solution(4992416151417636656)
XLA Ops:
  0.6 133.9 %layer.1 = (bf16[24,1024]{1,0:T(8,128)(2,1)}, bf16[24,1024]{1,0:T(8,128)(2,1)}, bf16[1024,896]{1,0:T(8,128)(2,1)}, bf16[1024,896]{1,0:T(8,128)(2,1)}, bf16[896,1024]{1,0:T(8,128)(2,1)}) custom-call(bf16[24,1024]{1,0:T(8,128)(2,1)} %tok_in.1, bf16[1024,896]{1,0:T(8,128)(2,1)} %gw_in.1, bf16[1024,896]{1,0:T(8,128)(2,1)} %uw_in.1, bf16[896,1024]{1,0:T(8,128)(2,1)} %dw_in.1, ...), custom_call_target="tpu_custom_call" | custom-call | flops 12683575296 | bytes 12582912 | tf_op jit(solution)/shard_map/layer/pallas_call | solution.py:383
  134.5 1.4 copy.18
  136.0 1.4 copy.19
  137.4 0.0 copy-start.1
  137.4 3.0 %copy.20 = bf16[1024,896]{1,0:T(8,128)(2,1)} copy(bf16[1024,896]{1,0:T(8,128)(2,1)} %get-tuple-element.12) | data formatting | bytes 3670016
  140.4 0.0 copy-done.1
  140.4 0.0 copy-start
  140.4 1.2 copy.21
  141.6 0.9 copy-done
  142.6 1.2 copy.22
Async XLA Ops:
  137.4 3.0 %copy-start.1 = (bf16[1024,896]{1,0:T(8,128)(2,1)S(1)}, bf16[1024,896]{1,0:T(8,128)(2,1)}, u32[]{:S(2)}) copy-start(bf16[1024,896]{1,0:T(8,128)(2,1)} %get-tuple-element.13) | copy-start | bytes 5505028
  140.4 2.2 %copy-start = (bf16[896,1024]{1,0:T(8,128)(2,1)S(1)}, bf16[896,1024]{1,0:T(8,128)(2,1)}, u32[]{:S(2)}) copy-start(bf16[896,1024]{1,0:T(8,128)(2,1)} %get-tuple-element.14) | copy-start | bytes 5505028

commit v2 on v0

v2 whole, which is shorter than its diff:
```python
import math

import jax
import jax.numpy as jnp
from jax import lax
from jax.experimental import pallas as pl
from jax.experimental.pallas import tpu as pltpu
from jax.sharding import PartitionSpec as P

MESH = pl.DeviceIdType.MESH
BF = jnp.bfloat16
F32 = jnp.float32

TOK = 768
W = 1024
FH = 896
OWN = 24
CH = 48
CA = 512
CS = (128, 256, 256, 128)
DZ = (0, 1, 7, 2, 4, 5, 3, 6)
YFIRST = (False, False, True, True)
ORDER = (
    ("ag", 0), ("mgu",), ("ag", 1), ("md",), ("agy", 0), ("agy", 1), ("asm", 0, 0), ("agz", 0, 1), ("asm", 1, 0),
    ("agz", 1, 1), ("asm", 0, 2), ("asm", 0, 1), ("gu", 0), ("asm", 1, 2), ("asm", 1, 1), ("hd", 0), ("agz", 0, 2),
    ("gu1", 0), ("agz", 1, 2), ("asm", 0, 3), ("gu", 1), ("asm", 0, 7), ("asm", 1, 7), ("agz", 0, 3), ("asm", 1, 3),
    ("hd1", 0), ("gu2", 0), ("asm", 0, 5), ("agz", 1, 3), ("hd", 1), ("asm", 0, 6), ("agz", 0, 4), ("gu1", 1),
    ("asm", 1, 5), ("asm", 1, 6), ("asm", 0, 4), ("agz", 1, 4), ("act", 0), ("gu", 2), ("hd2", 0), ("asm", 1, 4),
    ("gu2", 1), ("hx", 0), ("hd1", 1), ("hd", 2), ("gu1", 2), ("act2", 0), ("act", 1), ("hf", 0), ("hd2", 1),
    ("gu", 3), ("gu2", 2), ("pf", 0, 0), ("hd1", 2), ("hd", 3), ("act2", 1), ("hx", 1), ("py", 0), ("gu1", 3),
    ("d", 0, 0), ("hd2", 2), ("ea", 0, 0), ("act", 2), ("pf", 1, 0), ("hd1", 3), ("hf", 1), ("pf", 0, 1), ("py", 1),
    ("gu2", 3), ("act2", 2), ("hx", 2), ("hd2", 3), ("d", 1, 0), ("d", 0, 1), ("act", 3), ("ea", 1, 0), ("pf", 1, 1),
    ("py", 2), ("ea", 0, 1), ("pf", 2, 0), ("hf", 2), ("act2", 3), ("hx", 3), ("d", 1, 1), ("d", 0, 2), ("pf", 2, 1),
    ("py", 3), ("ea", 1, 1), ("ea", 0, 2), ("pf", 3, 0), ("hf", 3), ("d", 1, 2), ("pf", 3, 1), ("ea", 1, 2),
    ("d", 0, 3), ("eb", 0, 2), ("d", 1, 3), ("ea", 0, 3), ("wd",), ("eb", 1, 2), ("ea", 1, 3), ("wgp",), ("eb", 0, 3),
    ("f1", 0), ("eb", 1, 3), ("f1", 1), ("f2", 0), ("f2", 1),
)

NCH = len(CS)
OFF = [sum(CS[:j]) for j in range(NCH + 1)]
NEG = tuple(DZ.index((8 - d) % 8) for d in DZ)
SELF = DZ.index(0)
DONE = [o // 96 for o in OFF]


def dot_nn(a, b):
    return jnp.dot(a, b, preferred_element_type=F32)


def dot_nt(a, b):
    return lax.dot_general(a, b, (((1,), (1,)), ((), ())), preferred_element_type=F32)


def dot_tn(a, b):
    return lax.dot_general(a, b, (((0,), (0,)), ((), ())), preferred_element_type=F32)


def loop(n, body):
    for i in range(n):
        body(i)


def buffers():
    V = pltpu.VMEM
    b = dict(
        wcat=V((W, 2 * FH), BF), wd=V((FH, W), BF), io_buf=V((2, OWN, W), BF),
        slot_o=V((2, 8, 2, CH, 512), BF), slot_s=V((2, 8, 2, CH, 512), BF),
        tok=V((TOK, W), BF), cot=V((TOK, W), BF),
        p_gu=V((TOK, 2 * FH), BF), hid=V((TOK, FH), BF), gp=V((TOK, 2 * FH), BF),
        e_own=V((2, 2, 8, CH, 512), F32), e_sib=V((2, 2, 8, CH, 512), F32),
        e_sb=V((2, 2, 8, CH, 512), BF), e_sr=V((2, 2, 8, CH, 512), BF),
        ey_s=V((2, 8, CH, 512), BF), ey_r=V((2, 8, CH, 512), BF),
        ez_s=V((2, 8, 2, CH, 512), BF), ez_r=V((2, 8, 2, CH, 512), BF),
        ef_s=V((2, CH, 512), BF), ef_r=V((2, CH, 512), BF),
        gg_b=V((W, FH), BF), gu_b=V((W, FH), BF), gd_b=V((FH, W), BF),
    )
    for j, r in enumerate(CS):
        pr, xr = r // 8, r // 4
        b.update({
            ("p_h", j): V((4, 2, pr, FH), BF), ("fy_h", j): V((4, pr, FH), BF),
            ("f1g", j): V((xr, FH), BF), ("f1u", j): V((xr, FH), BF),
            ("f2g", j): V((2, xr, FH), BF), ("f2u", j): V((2, xr, FH), BF),
            ("own_gu", j): V((pr, 2 * FH), F32), ("sy_gu", j): V((pr, 2 * FH), BF),
            ("fy_gu", j): V((pr, 2 * FH), BF),
            ("f1a", j): V((pr, CA), BF), ("f1b", j): V((pr, FH - CA), BF),
            ("f2h", j): V((2, pr, FH), BF),
        })
    return b


def kernel(*refs):
    (tok_in, gw_in, uw_in, dw_in, gm, um, dm, cot_in, mix_out, gt_out, gg_out, gu_out, gd_out) = refs[:13]
    b = dict(zip(buffers(), refs[13:-3]))
    lsem, ssem, rsem = refs[-3:]
    wcat, wd, io_buf, slot_o, slot_s = (b[k] for k in ("wcat", "wd", "io_buf", "slot_o", "slot_s"))
    tok, cot, p_gu, hid, gp = (b[k] for k in ("tok", "cot", "p_gu", "hid", "gp"))
    e_own, e_sib, e_sb, e_sr = (b[k] for k in ("e_own", "e_sib", "e_sb", "e_sr"))

    s = lax.axis_index("seq")
    m = lax.axis_index("mp")
    h, x = s // 4, s % 4
    l, z, c = m // 16, (m // 2) % 8, m % 2
    xr, xl, xf = (x + 1) % 4, (x + 3) % 4, (x + 2) % 4
    oh = 1 - h

    def mp_of(dz, dl, dc=0):
        return ((l + dl) % 2) * 16 + ((z + dz) % 8) * 2 + (c + dc) % 2

    RIGHT, LEFT, YH = (h * 4 + xr, m), (h * 4 + xl, m), (oh * 4 + x, m)
    SIB, YL = (s, mp_of(0, 0, 1)), (s, mp_of(0, 1))

    def ZL(dz):
        return (s, mp_of(dz, 0))

    sent, waited = {}, set()

    def send(key, src, dst, to):
        k = len(sent)
        d = pltpu.make_async_remote_copy(
            src_ref=src, dst_ref=dst, send_sem=ssem.at[k], recv_sem=rsem.at[k],
            device_id=to, device_id_type=MESH,
        )
        d.start()
        sent[key] = d

    def got(*keys):
        for key in keys:
            if key not in waited:
                waited.add(key)
                sent[key].wait_recv()

    loads = [
        pltpu.make_async_copy(tok_in, io_buf.at[0], lsem.at[0]),
        pltpu.make_async_copy(cot_in, io_buf.at[1], lsem.at[1]),
        pltpu.make_async_copy(gw_in, wcat.at[:, pl.ds(0, FH)], lsem.at[2]),
        pltpu.make_async_copy(uw_in, wcat.at[:, pl.ds(FH, FH)], lsem.at[3]),
        pltpu.make_async_copy(dw_in, wd, lsem.at[4]),
    ]
    for d in loads:
        d.start()
    stores = []

    barrier = pltpu.get_barrier_semaphore()
    peers = [RIGHT, LEFT, YH, SIB, YL] + [ZL(dz) for dz in range(1, 8)]
    for to in peers:
        pl.semaphore_signal(barrier, inc=1, device_id=to, device_id_type=MESH)

    def pack(v):
        v = v.astype(F32)
        return jnp.concatenate([v[:, :512], v[:, 512:]], axis=0).astype(BF)

    def unpack(v):
        v = v.astype(F32)
        return jnp.concatenate([v[:OWN], v[OWN:]], axis=1)

    for a in range(2):
        loads[a].wait()
        slot_o[a, SELF, 0] = pack(io_buf[a])
    pl.semaphore_wait(barrier, len(peers))

    def at(dz):
        return DZ.index(dz % 8)

    def hop_r(a, d, dl):
        send(("r", a, d, dl), slot_o.at[a, at(1 - d), dl], slot_o.at[a, at(-d), dl], ZL(1))

    def hop_l(a, d, dl):
        send(("l", a, d, dl), slot_o.at[a, at(d - 1), dl], slot_o.at[a, at(d), dl], ZL(7))

    def t_ag(a):
        send(("yl", a), slot_o.at[a, SELF, 0], slot_o.at[a, SELF, 1], YL)
        hop_r(a, 1, 0)
        hop_l(a, 1, 0)

    def t_agy(a):
        got(("yl", a))
        hop_r(a, 1, 1)
        hop_l(a, 1, 1)
        send(("sh", a, SELF), slot_o.at[a, SELF], slot_s.at[a, SELF], SIB)

    def t_agz(a, d):
        for dl in range(2):
            if d < 4 or dl == 0:
                got(("r", a, d, dl))
            if d < 3 or (d == 3 and dl == 0):
                hop_r(a, d + 1, dl)
            if d < 4 or dl == 1:
                got(("l", a, d, dl))
            if d < 3 or (d == 3 and dl == 1):
                hop_l(a, d + 1, dl)
        for q in (at(-d), at(d))[: 2 if d < 4 else 1]:
            send(("sh", a, q), slot_o.at[a, q], slot_s.at[a, q], SIB)

    def t_asm(a, q):
        got(("sh", a, q))
        ref = (tok, cot)[a]
        for dl in range(2):
            v = jnp.concatenate([unpack(slot_o[a, q, dl]), unpack(slot_s[a, q, dl])], axis=0)
            ref[pl.ds(q * 96 + dl * CH, CH), :] = v.astype(BF)

    def masked(ref, mask, rows, cols, col0):
        def body(i):
            r = pl.ds(i * 128, 128)
            for k in range(cols):
                cs = pl.ds(col0 + k * 128, 128)
                ref[r, cs] = (ref[r, cs].astype(F32) * mask[i, k].astype(F32)).astype(BF)
        loop(rows, body)

    def t_mgu():
        loads[2].wait()
        masked(wcat, gm, 8, 7, 0)
        loads[3].wait()
        masked(wcat, um, 8, 7, FH)

    def t_md():
        loads[4].wait()
        masked(wd, dm, 7, 8, 0)

    def rows_x(j, xi):
        return pl.ds(pl.multiple_of(OFF[j] + xi * (CS[j] // 4), CS[j] // 4), CS[j] // 4)

    def rows_p(j, xi, hi):
        return pl.ds(pl.multiple_of(OFF[j] + xi * (CS[j] // 4) + hi * (CS[j] // 8), CS[j] // 8), CS[j] // 8)

    G, U = pl.ds(0, FH), pl.ds(FH, FH)
    A, B = pl.ds(0, CA), pl.ds(CA, FH - CA)

    def t_gu(j):
        rows = pl.ds(OFF[j], CS[j])

        def body(n):
            cs = pl.ds(n * 256, 256)
            p_gu[rows, cs] = dot_nn(tok[rows, :], wcat[:, cs]).astype(BF)
        loop(7, body)
        send(("g1", j), p_gu.at[rows_x(j, xf), G], b["f1g", j], RIGHT)
        send(("u1", j), p_gu.at[rows_x(j, xf), U], b["f1u", j], LEFT)
        send(("g2l", j), p_gu.at[rows_x(j, xl), G], b["f2g", j].at[1], LEFT)
        send(("u2r", j), p_gu.at[rows_x(j, xr), U], b["f2u", j].at[0], RIGHT)

    def t_hd(j):
        rows, p_h, pr = pl.ds(OFF[j], CS[j]), b["p_h", j], CS[j] // 8

        def body(n):
            cs = pl.ds(n * 256, 256)
            p_h[:, :, :, cs] = dot_nt(cot[rows, :], wd[cs, :]).astype(BF).reshape(4, 2, pr, 256)
        loop(3, body)
        cs = pl.ds(768, 128)
        p_h[:, :, :, cs] = dot_nt(cot[rows, :], wd[cs, :]).astype(BF).reshape(4, 2, pr, 128)
        send(("hy", j), p_h.at[:, oh], b["fy_h", j], YH)

    def add_to(ref, at_, other):
        ref[at_] = (ref[at_].astype(F32) + other[...].astype(F32)).astype(BF)

    def t_gu1(j):
        got(("g1", j))
        rows = rows_x(j, xr)
        add_to(p_gu, (rows, G), b["f1g", j])
        send(("g2r", j), p_gu.at[rows, G], b["f2g", j].at[0], RIGHT)
        got(("u1", j))
        rows = rows_x(j, xl)
        add_to(p_gu, (rows, U), b["f1u", j])
        send(("u2l", j), p_gu.at[rows, U], b["f2u", j].at[1], LEFT)

    def t_hd1(j):
        p_h, f2h = b["p_h", j], b["f2h", j]
        got(("hy", j))
        for xi in range(4):
            add_to(p_h, (xi, h), b["fy_h", j].at[xi])
        send(("h1a", j), p_h.at[xf, h, :, A], b["f1a", j], RIGHT)
        send(("h1b", j), p_h.at[xf, h, :, B], b["f1b", j], LEFT)
        send(("h2rb", j), p_h.at[xr, h, :, B], f2h.at[0, :, B], RIGHT)
        send(("h2la", j), p_h.at[xl, h, :, A], f2h.at[1, :, A], LEFT)

    def t_hd2(j):
        p_h, f2h = b["p_h", j], b["f2h", j]
        got(("h1a", j))
        add_to(p_h, (xr, h, slice(None), A), b["f1a", j])
        send(("h2ra", j), p_h.at[xr, h, :, A], f2h.at[0, :, A], RIGHT)
        got(("h1b", j))
        add_to(p_h, (xl, h, slice(None), B), b["f1b", j])
        send(("h2lb", j), p_h.at[xl, h, :, B], f2h.at[1, :, B], LEFT)

    def t_gu2(j):
        pr = CS[j] // 8
        got(("g2l", j), ("u2r", j), ("g2r", j), ("u2l", j))
        for f2, cs in ((b["f2g", j], G), (b["f2u", j], U)):
            def total(hi):
                r = pl.ds(pl.multiple_of(hi * pr, pr), pr)
                return p_gu[rows_p(j, x, hi), cs].astype(F32) + f2[0, r, :].astype(F32) + f2[1, r, :].astype(F32)
            b["sy_gu", j][:, cs] = total(oh).astype(BF)
            b["own_gu", j][:, cs] = total(h)
        send(("guy", j), b["sy_gu", j], b["fy_gu", j], YH)

    def steps(j, body):
        def at_(i):
            r = pl.ds(i * 16, 16)
            rr = pl.ds(pl.multiple_of(OFF[j] + x * (CS[j] // 4) + h * (CS[j] // 8) + i * 16, 16), 16)
            body(r, rr)
        loop(CS[j] // 128, at_)

    def t_act(j):
        got(("guy", j))
        own_gu, fy_gu = b["own_gu", j], b["fy_gu", j]

        def body(r, rr):
            pre_gate = own_gu[r, G] + fy_gu[r, G].astype(F32)
            pre_up = own_gu[r, U] + fy_gu[r, U].astype(F32)
            own_gu[r, G] = pre_gate
            own_gu[r, U] = pre_up
            hid[rr, :] = (pre_gate * jax.nn.sigmoid(pre_gate) * pre_up).astype(BF)
        steps(j, body)
        mine = rows_p(j, x, h)
        send(("hr", j), hid.at[mine], hid.at[mine], RIGHT)
        send(("hl", j), hid.at[mine], hid.at[mine], LEFT)
        send(("hy0", j), hid.at[mine], hid.at[mine], YH)

    def t_act2(j):
        got(("h2rb", j), ("h2la", j), ("h2ra", j), ("h2lb", j))
        own_gu, p_h, f2h = b["own_gu", j], b["p_h", j], b["f2h", j]

        def body(r, rr):
            pre_gate, pre_up = own_gu[r, G], own_gu[r, U]
            grad_hidden = p_h[x, h, r, :].astype(F32) + f2h[0, r, :].astype(F32) + f2h[1, r, :].astype(F32)
            sig = jax.nn.sigmoid(pre_gate)
            gp[rr, G] = (grad_hidden * pre_up * sig * (1.0 + pre_gate * (1.0 - sig))).astype(BF)
            gp[rr, U] = (grad_hidden * (pre_gate * sig)).astype(BF)
        steps(j, body)
        mine = rows_p(j, x, h)
        send(("py", j), gp.at[mine], gp.at[mine], YH)
        send(("pr0", j), gp.at[mine], gp.at[mine], RIGHT)
        send(("pl0", j), gp.at[mine], gp.at[mine], LEFT)

    def t_hx(j):
        fl, fr = rows_p(j, xl, h), rows_p(j, xr, h)
        got(("hr", j))
        send(("hfr", j), hid.at[fl, A], hid.at[fl, A], RIGHT)
        got(("hl", j))
        send(("hfl", j), hid.at[fr, B], hid.at[fr, B], LEFT)
        send(("hyl", j), hid.at[fl], hid.at[fl], YH)
        send(("hyr", j), hid.at[fr], hid.at[fr], YH)

    def t_hf(j):
        got(("hfr", j), ("hfl", j))
        ff = rows_p(j, xf, h)
        send(("hyf", j), hid.at[ff], hid.at[ff], YH)

    def t_py(j):
        got(("py", j))
        other = rows_p(j, x, oh)
        send(("pr1", j), gp.at[other], gp.at[other], RIGHT)
        send(("pl1", j), gp.at[other], gp.at[other], LEFT)

    def t_pf(j, k):
        fl, fr = rows_p(j, xl, (h, oh)[k]), rows_p(j, xr, (h, oh)[k])
        got((("pr0", "pr1")[k], j))
        send(("pfr", j, k), gp.at[fl, G], gp.at[fl, G], RIGHT)
        got((("pl0", "pl1")[k], j))
        send(("pfl", j, k), gp.at[fr, U], gp.at[fr, U], LEFT)

    def t_d(a, j):
        if a == 0:
            got(("hy0", j), ("hyl", j), ("hyr", j), ("hyf", j))
        else:
            got(("pfr", j, 0), ("pfl", j, 0), ("pfr", j, 1), ("pfl", j, 1))
        p0, p1 = DONE[j], DONE[j + 1]
        n_p = p1 - p0
        rows = pl.ds(p0 * 96, n_p * 96)

        def body(n):
            cs = pl.ds(n * 256, 256)
            er = pl.ds((n // 2) * OWN, OWN)
            ec = pl.ds((n % 2) * 256, 256)
            v = dot_nn(hid[rows, :], wd[:, cs]) if a == 0 else dot_nt(gp[rows, :], wcat[cs, :])
            v = v.reshape(n_p, 2, 2, OWN, 256)
            for p in range(n_p):
                for dl in range(2):
                    e_own[a, dl, p0 + p, er, ec] = v[p, dl, 0]
                    e_sib[a, dl, p0 + p, er, ec] = v[p, dl, 1]
        loop(4, body)
        for dl in (1, 0):
            for p in range(p0, p1):
                e_sb[a, dl, p] = e_sib[a, dl, p].astype(BF)
            ps = pl.ds(p0, n_p)
            send(("es", a, j, dl), e_sb.at[a, dl, ps], e_sr.at[a, dl, ps], SIB)

    def to_z(a, p, dl, v):
        if p == SELF:
            e_own[a, dl, p] = v
        else:
            b["ez_s"][a, p, dl] = v.astype(BF)
            send(("ez", a, p, dl), b["ez_s"].at[a, p, dl], b["ez_r"].at[a, p, dl], ZL(DZ[p]))

    def t_ea(a, j):
        p0, p1 = DONE[j], DONE[j + 1]
        if YFIRST[j]:
            got(("es", a, j, 1))
            for p in range(p0, p1):
                b["ey_s"][a, p] = (e_own[a, 1, p] + e_sr[a, 1, p].astype(F32)).astype(BF)
            ps = pl.ds(p0, p1 - p0)
            send(("ey", a, j), b["ey_s"].at[a, ps], b["ey_r"].at[a, ps], YL)
        else:
            for dl in (1, 0):
                got(("es", a, j, dl))
                for p in range(p0, p1):
                    to_z(a, p, dl, e_own[a, dl, p] + e_sr[a, dl, p].astype(F32))

    def t_eb(a, j):
        got(("es", a, j, 0), ("ey", a, j))
        for p in range(DONE[j], DONE[j + 1]):
            to_z(a, p, 0, e_own[a, 0, p] + e_sr[a, 0, p].astype(F32) + b["ey_r"][a, p].astype(F32))

    ZF = [p for j in range(NCH) for p in range(DONE[j], DONE[j + 1]) if not YFIRST[j]]

    def whole(a, dl, pairs):
        v = e_own[a, dl, SELF] if SELF in pairs else None
        for p in pairs:
            if p != SELF:
                got(("ez", a, p, dl))
                t = b["ez_r"][a, p, dl].astype(F32)
                v = t if v is None else v + t
        return v

    def t_f1(a):
        b["ef_s"][a] = whole(a, 1, ZF).astype(BF)
        send(("ef", a), b["ef_s"].at[a], b["ef_r"].at[a], YL)

    def t_f2(a):
        v = whole(a, 0, range(8))
        if ZF:
            got(("ef", a))
            v = v + b["ef_r"][a].astype(F32)
        (mix_out, gt_out)[a][...] = jnp.concatenate([v[:OWN], v[OWN:]], axis=1).astype(BF)

    scale = 1.0 / math.sqrt(TOK)

    def store(k, src, dst):
        d = pltpu.make_async_copy(src, dst, lsem.at[k])
        d.start()
        stores.append(d)

    def t_wgp():
        def body(i):
            cs = pl.ds(i * 128, 128)
            v = dot_tn(tok[:, cs], gp[...]) * scale
            for k in range(7):
                ks = pl.ds(k * 128, 128)
                b["gg_b"][cs, ks] = (v[:, k * 128:(k + 1) * 128] * gm[i, k].astype(F32)).astype(BF)
                b["gu_b"][cs, ks] = (v[:, FH + k * 128:FH + (k + 1) * 128] * um[i, k].astype(F32)).astype(BF)
        loop(8, body)
        store(0, b["gg_b"], gg_out)
        store(1, b["gu_b"], gu_out)

    def t_wd():
        def body(i):
            cs = pl.ds(i * 128, 128)
            v = dot_tn(hid[:, cs], cot[...]) * scale
            for k in range(8):
                ks = pl.ds(k * 128, 128)
                b["gd_b"][cs, ks] = (v[:, k * 128:(k + 1) * 128] * dm[i, k].astype(F32)).astype(BF)
        loop(7, body)
        store(2, b["gd_b"], gd_out)

    do = dict(
        ag=t_ag, agy=t_agy, agz=t_agz, asm=t_asm, mgu=t_mgu, md=t_md, gu=t_gu, hd=t_hd, gu1=t_gu1, hd1=t_hd1, hd2=t_hd2,
        gu2=t_gu2, act=t_act, act2=t_act2, hx=t_hx, hf=t_hf, py=t_py, pf=t_pf, d=t_d, ea=t_ea, eb=t_eb, f1=t_f1, f2=t_f2,
        wgp=t_wgp, wd=t_wd,
    )
    for name, *which in ORDER:
        do[name](*which)
    for d in list(sent.values()):
        d.wait_send()
    for d in stores:
        d.wait()


def hand_on(*refs):
    ins, outs, held, (in_sem, out_sem) = refs[:5], refs[5:10], refs[10:15], refs[15:]
    reads, writes = [], []
    for k in (2, 3, 4, 0, 1):
        n = 4 if ins[k].shape[0] > OWN else 1
        for i in range(n):
            r = pl.ds(i * (ins[k].shape[0] // n), ins[k].shape[0] // n)
            t = len(reads)
            reads.append(pltpu.make_async_copy(ins[k].at[r], held[k].at[r], in_sem.at[t]))
            writes.append(pltpu.make_async_copy(held[k].at[r], outs[k].at[r], out_sem.at[t]))
            reads[t].start()
    for read, write in zip(reads, writes):
        read.wait()
        write.start()
    for write in writes:
        write.wait()


def on_device(tokens, gate_weight, up_weight, down_weight, gate_mask, up_mask, down_mask, grad_out):
    vm = pl.BlockSpec(memory_space=pltpu.VMEM)
    sm = pl.BlockSpec(memory_space=pltpu.SMEM)
    hbm = pl.BlockSpec(memory_space=pl.ANY)
    n_msg = 46 + NCH * 37 + 2 * 14 + 2
    D, V = pltpu.SemaphoreType.DMA, pltpu.VMEM
    outs = pl.pallas_call(
        kernel,
        out_shape=(
            jax.ShapeDtypeStruct((OWN, W), BF),
            jax.ShapeDtypeStruct((OWN, W), BF),
            jax.ShapeDtypeStruct((W, FH), BF),
            jax.ShapeDtypeStruct((W, FH), BF),
            jax.ShapeDtypeStruct((FH, W), BF),
        ),
        in_specs=[hbm, hbm, hbm, hbm, sm, sm, sm, hbm],
        out_specs=(vm, vm, hbm, hbm, hbm),
        scratch_shapes=[*buffers().values(), D((5,)), D((n_msg,)), D((n_msg,))],
        name="layer",
        compiler_params=pltpu.CompilerParams(
            collective_id=0, has_side_effects=True, vmem_limit_bytes=60 << 20
        ),
        cost_estimate=pl.CostEstimate(flops=9 * 2 * TOK * W * FH, bytes_accessed=12 << 20, transcendentals=TOK * FH),
    )(tokens, gate_weight, up_weight, down_weight, gate_mask, up_mask, down_mask, grad_out)
    return pl.pallas_call(
        hand_on,
        out_shape=tuple(jax.ShapeDtypeStruct(o.shape, o.dtype) for o in outs),
        in_specs=[hbm] * 5,
        out_specs=(hbm,) * 5,
        scratch_shapes=[V(o.shape, o.dtype) for o in outs] + [D((14,)), D((14,))],
        name="hand_on",
        compiler_params=pltpu.CompilerParams(vmem_limit_bytes=60 << 20),
        cost_estimate=pl.CostEstimate(flops=0, bytes_accessed=12 << 20, transcendentals=0),
    )(*outs)


def solution(mesh):
    placed = (
        P("mp", "seq"),
        P("seq", "mp"),
        P("seq", "mp"),
        P("mp", "seq"),
        P("seq", "mp"),
        P("seq", "mp"),
        P("mp", "seq"),
        P("mp", "seq"),
    )
    return jax.shard_map(
        on_device,
        mesh=mesh,
        in_specs=placed,
        out_specs=(P("mp", "seq"), P("mp", "seq"), P("seq", "mp"), P("seq", "mp"), P("mp", "seq")),
        check_vma=False,
    )
```

time: 520 us -> 109 us (0.21)
  waiting for transfers between devices: 438 us -> 0 us
  Pallas kernels: 0 us -> 108 us
  matrix products: 37.1 us -> 0 us
  local copies, waits for them, and re-layouts: 22.5 us -> 0 us
  between operations: 14 us -> 0.8 us
    reduce_scatter x2 -> x0, waiting for transfers between devices: 205 us -> none  [the longest x1 117 us: on_device(): lax.psum_scatter(jnp.dot(hidden, w_down, preferred_element_type=jnp.float...]
    all_gather x2 -> x0, waiting for transfers between devices: 118 us -> none  [the longest x1 61.7 us: on_device(): inputs_all = lax.all_gather(tokens, 'mp', axis=0, tiled=True)]
    psum x1 -> x0, waiting for transfers between devices: 114 us -> none  [on_device(): lax.psum(part_up.astype(jnp.bfloat16), 'seq').astype(jnp.float32)]
    pallas_call x0 -> x2, Pallas kernels: none -> 108 us  [the longest x1 103 us: on_device(): pl.pallas_call(kernel, out_shape=(jax.ShapeDtypeStruct((OWN, W), BF), jax...]
    dot_general x9 -> x0, matrix products: 37.1 us -> none  [the longest x3 14 us: inner_right(): lax.dot_general(left, right, (((1,), (1,)), ((), ())), preferred_element_...]
    unnamed x44 -> x0, local copies, waits for them, and re-layouts: 20.3 us -> none
  transfers between devices with their start and end apart: 5 -> 0, of which waited for: 5 -> 0; matrix products, arithmetic and copies ran while one was open for 8% -> 0% of each run, Pallas kernels for 0% -> 0%
where the time goes in v2:
time: 109 us
  Pallas kernels  108 us (99%)
    pallas_call x1, Pallas kernels, on_device(): pl.pallas_call(kernel, out_shape=(jax.ShapeDtypeStruct((OWN, W), BF), jax...  103 us
    pallas_call x1, Pallas kernels, on_device(): pl.pallas_call(hand_on, out_shape=tuple((jax.ShapeDtypeStruct(o.shape, o....  5.07 us

profile of v2, /device:TPU:1, one launch (start us, length us, event | category | flops | bytes accessed | tf_op | source)
XLA Modules:
  0.0 108.9 jit_solution(5356317292124144376)
XLA Ops:
  0.6 103.0 %layer.1 = (bf16[24,1024]{1,0:T(8,128)(2,1)}, bf16[24,1024]{1,0:T(8,128)(2,1)}, bf16[1024,896]{1,0:T(8,128)(2,1)}, bf16[1024,896]{1,0:T(8,128)(2,1)}, bf16[896,1024]{1,0:T(8,128)(2,1)}) custom-call(bf16[24,1024]{1,0:T(8,128)(2,1)} %refs_0_.1, bf16[1024,896]{1,0:T(8,128)(2,1)} %refs_1_.1, bf16[1024,896]{1,0:T(8,128)(2,1)} %refs_2_.1, ...), custom_call_target="tpu_custom_call" | custom-call | flops 12683575296 | bytes 12582912 | tf_op jit(solution)/shard_map/layer/pallas_call | solution.py:500
  103.7 5.1 %hand_on.1 = (bf16[24,1024]{1,0:T(8,128)(2,1)}, bf16[24,1024]{1,0:T(8,128)(2,1)}, bf16[1024,896]{1,0:T(8,128)(2,1)}, bf16[1024,896]{1,0:T(8,128)(2,1)}, bf16[896,1024]{1,0:T(8,128)(2,1)}) custom-call(bf16[24,1024]{1,0:T(8,128)(2,1)} %get-tuple-element.10.refs_0_, bf16[24,1024]{1,0:T(8,128)(2,1)} %get-tuple-element.11.refs_1_, ...), custom_call_target="tpu_custom_call" | custom-call | bytes 12582912 | tf_op jit(solution)/shard_map/hand_on/pallas_call | solution.py:518

commit v3 on v2

--- a/solution.py
+++ b/solution.py
@@ -18,22 +18,23 @@
 CH = 48
 CA = 512
 CS = (128, 256, 256, 128)
-DZ = (0, 1, 7, 2, 4, 5, 3, 6)
+DZ = (1, 0, 7, 2, 4, 5, 3, 6)
 YFIRST = (False, False, True, True)
 ORDER = (
-    ("ag", 0), ("mgu",), ("ag", 1), ("md",), ("agy", 0), ("agy", 1), ("asm", 0, 0), ("agz", 0, 1), ("asm", 1, 0),
-    ("agz", 1, 1), ("asm", 0, 2), ("asm", 0, 1), ("gu", 0), ("asm", 1, 2), ("asm", 1, 1), ("hd", 0), ("agz", 0, 2),
-    ("gu1", 0), ("agz", 1, 2), ("asm", 0, 3), ("gu", 1), ("asm", 0, 7), ("asm", 1, 7), ("agz", 0, 3), ("asm", 1, 3),
-    ("hd1", 0), ("gu2", 0), ("asm", 0, 5), ("agz", 1, 3), ("hd", 1), ("asm", 0, 6), ("agz", 0, 4), ("gu1", 1),
-    ("asm", 1, 5), ("asm", 1, 6), ("asm", 0, 4), ("agz", 1, 4), ("act", 0), ("gu", 2), ("hd2", 0), ("asm", 1, 4),
-    ("gu2", 1), ("hx", 0), ("hd1", 1), ("hd", 2), ("gu1", 2), ("act2", 0), ("act", 1), ("hf", 0), ("hd2", 1),
-    ("gu", 3), ("gu2", 2), ("pf", 0, 0), ("hd1", 2), ("hd", 3), ("act2", 1), ("hx", 1), ("py", 0), ("gu1", 3),
-    ("d", 0, 0), ("hd2", 2), ("ea", 0, 0), ("act", 2), ("pf", 1, 0), ("hd1", 3), ("hf", 1), ("pf", 0, 1), ("py", 1),
-    ("gu2", 3), ("act2", 2), ("hx", 2), ("hd2", 3), ("d", 1, 0), ("d", 0, 1), ("act", 3), ("ea", 1, 0), ("pf", 1, 1),
-    ("py", 2), ("ea", 0, 1), ("pf", 2, 0), ("hf", 2), ("act2", 3), ("hx", 3), ("d", 1, 1), ("d", 0, 2), ("pf", 2, 1),
-    ("py", 3), ("ea", 1, 1), ("ea", 0, 2), ("pf", 3, 0), ("hf", 3), ("d", 1, 2), ("pf", 3, 1), ("ea", 1, 2),
-    ("d", 0, 3), ("eb", 0, 2), ("d", 1, 3), ("ea", 0, 3), ("wd",), ("eb", 1, 2), ("ea", 1, 3), ("wgp",), ("eb", 0, 3),
-    ("f1", 0), ("eb", 1, 3), ("f1", 1), ("f2", 0), ("f2", 1),
+    ("ag", 0), ("md",), ("ag", 1), ("mgu",), ("agy", 0), ("agy", 1), ("agz", 0, 1), ("asm", 0, 1), ("agz", 1, 1),
+    ("asm", 0, 0), ("gu", 0), ("asm", 1, 2), ("agz", 0, 2), ("asm", 1, 0), ("asm", 0, 2), ("asm", 1, 1), ("hd", 0),
+    ("agz", 1, 2), ("gu1", 0), ("asm", 0, 3), ("gu", 1), ("asm", 1, 3), ("agz", 0, 3), ("hd", 1), ("agz", 1, 3),
+    ("asm", 0, 6), ("hd1", 0), ("gu2", 0), ("asm", 1, 7), ("agz", 0, 4), ("gu1", 1), ("asm", 1, 6), ("asm", 0, 5),
+    ("agz", 1, 4), ("asm", 0, 4), ("gu", 2), ("asm", 1, 5), ("asm", 1, 4), ("hd", 2), ("hd2", 0), ("hd1", 1),
+    ("gu2", 1), ("gu1", 2), ("hd", 3), ("act", 0), ("act2", 0), ("asm", 0, 7), ("gu", 3), ("gu2", 2), ("hx", 0),
+    ("act", 1), ("hd2", 1), ("hd1", 2), ("gu1", 3), ("hf", 0), ("hx", 1), ("hd1", 3), ("hd2", 2), ("act2", 1),
+    ("hf", 1), ("act", 2), ("py", 0), ("gu2", 3), ("d", 0, 0), ("act2", 2), ("hx", 2), ("py", 1), ("pf", 0, 1),
+    ("d", 0, 1), ("hd2", 3), ("ea", 0, 0), ("hf", 2), ("pf", 0, 0), ("act", 3), ("pf", 1, 0), ("pf", 1, 1),
+    ("ea", 0, 1), ("py", 2), ("d", 1, 0), ("hx", 3), ("act2", 3), ("pf", 2, 0), ("d", 0, 2), ("d", 1, 1),
+    ("pf", 2, 1), ("ea", 1, 0), ("ea", 0, 2), ("pf", 3, 0), ("py", 3), ("hf", 3), ("ea", 1, 1), ("d", 1, 2),
+    ("pf", 3, 1), ("eb", 0, 2), ("ea", 1, 2), ("d", 0, 3), ("d", 1, 3), ("ea", 0, 3), ("eb", 1, 2), ("wgp", 3),
+    ("ea", 1, 3), ("eb", 0, 3), ("wd", 0), ("eb", 1, 3), ("f1", 1), ("wd", 1), ("f1", 0), ("wgp", 2), ("wd", 3),
+    ("wgp", 0), ("wd", 2), ("f2", 0), ("wgp", 1), ("f2", 1),
 )
 
 NCH = len(CS)
@@ -109,10 +110,10 @@
     RIGHT, LEFT, YH = (h * 4 + xr, m), (h * 4 + xl, m), (oh * 4 + x, m)
     SIB, YL = (s, mp_of(0, 0, 1)), (s, mp_of(0, 1))
 
-    def ZL(dz):
-        return (s, mp_of(dz, 0))
-
-    sent, waited = {}, set()
+    def ZL(dz, dl=0):
+        return (s, mp_of(dz, dl))
+
+    sent, waited, leaving = {}, set(), []
 
     def send(key, src, dst, to):
         k = len(sent)
@@ -122,8 +123,11 @@
         )
         d.start()
         sent[key] = d
+        leaving.append(d)
 
     def got(*keys):
+        while len(leaving) > 40:
+            leaving.pop(0).wait_send()
         for key in keys:
             if key not in waited:
                 waited.add(key)
@@ -141,7 +145,7 @@
     stores = []
 
     barrier = pltpu.get_barrier_semaphore()
-    peers = [RIGHT, LEFT, YH, SIB, YL] + [ZL(dz) for dz in range(1, 8)]
+    peers = [RIGHT, LEFT, YH, SIB, YL, ZL(1, 1), ZL(7, 1)] + [ZL(dz) for dz in range(1, 8)]
     for to in peers:
         pl.semaphore_signal(barrier, inc=1, device_id=to, device_id_type=MESH)
 
@@ -169,13 +173,12 @@
 
     def t_ag(a):
         send(("yl", a), slot_o.at[a, SELF, 0], slot_o.at[a, SELF, 1], YL)
-        hop_r(a, 1, 0)
-        hop_l(a, 1, 0)
+        for dl, right, left in ((0, ZL(1), ZL(7)), (1, ZL(1, 1), ZL(7, 1))):
+            send(("r", a, 1, dl), slot_o.at[a, SELF, 0], slot_o.at[a, at(7), dl], right)
+            send(("l", a, 1, dl), slot_o.at[a, SELF, 0], slot_o.at[a, at(1), dl], left)
 
     def t_agy(a):
         got(("yl", a))
-        hop_r(a, 1, 1)
-        hop_l(a, 1, 1)
         send(("sh", a, SELF), slot_o.at[a, SELF], slot_s.at[a, SELF], SIB)
 
     def t_agz(a, d):
@@ -433,32 +436,31 @@
 
     scale = 1.0 / math.sqrt(TOK)
 
-    def store(k, src, dst):
-        d = pltpu.make_async_copy(src, dst, lsem.at[k])
+    def store(k, src, dst, rows):
+        d = pltpu.make_async_copy(src.at[rows], dst.at[rows], lsem.at[k])
         d.start()
         stores.append(d)
 
-    def t_wgp():
-        def body(i):
+    def t_wgp(n):
+        for i in (2 * n, 2 * n + 1):
             cs = pl.ds(i * 128, 128)
             v = dot_tn(tok[:, cs], gp[...]) * scale
             for k in range(7):
                 ks = pl.ds(k * 128, 128)
                 b["gg_b"][cs, ks] = (v[:, k * 128:(k + 1) * 128] * gm[i, k].astype(F32)).astype(BF)
                 b["gu_b"][cs, ks] = (v[:, FH + k * 128:FH + (k + 1) * 128] * um[i, k].astype(F32)).astype(BF)
-        loop(8, body)
-        store(0, b["gg_b"], gg_out)
-        store(1, b["gu_b"], gu_out)
-
-    def t_wd():
-        def body(i):
+        store(3 * n, b["gg_b"], gg_out, pl.ds(n * 256, 256))
+        store(3 * n + 1, b["gu_b"], gu_out, pl.ds(n * 256, 256))
+
+    def t_wd(n):
+        blocks = range(2 * n, min(2 * n + 2, 7))
+        for i in blocks:
             cs = pl.ds(i * 128, 128)
             v = dot_tn(hid[:, cs], cot[...]) * scale
             for k in range(8):
                 ks = pl.ds(k * 128, 128)
                 b["gd_b"][cs, ks] = (v[:, k * 128:(k + 1) * 128] * dm[i, k].astype(F32)).astype(BF)
-        loop(7, body)
-        store(2, b["gd_b"], gd_out)
+        store(3 * n + 2, b["gd_b"], gd_out, pl.ds(n * 256, len(blocks) * 128))
 
     do = dict(
         ag=t_ag, agy=t_agy, agz=t_agz, asm=t_asm, mgu=t_mgu, md=t_md, gu=t_gu, hd=t_hd, gu1=t_gu1, hd1=t_hd1, hd2=t_hd2,
@@ -467,7 +469,7 @@
     )
     for name, *which in ORDER:
         do[name](*which)
-    for d in list(sent.values()):
+    for d in leaving:
         d.wait_send()
     for d in stores:
         d.wait()
@@ -508,7 +510,7 @@
         ),
         in_specs=[hbm, hbm, hbm, hbm, sm, sm, sm, hbm],
         out_specs=(vm, vm, hbm, hbm, hbm),
-        scratch_shapes=[*buffers().values(), D((5,)), D((n_msg,)), D((n_msg,))],
+        scratch_shapes=[*buffers().values(), D((12,)), D((n_msg,)), D((n_msg,))],
         name="layer",
         compiler_params=pltpu.CompilerParams(
             collective_id=0, has_side_effects=True, vmem_limit_bytes=60 << 20

time: 109 us -> 108 us (level)
  no operation moved by 1% of the time
where the time goes in v3:
time: 108 us
  Pallas kernels  107 us (99%)
    pallas_call x1, Pallas kernels, on_device(): pl.pallas_call(kernel, out_shape=(jax.ShapeDtypeStruct((OWN, W), BF), jax...  102 us
    pallas_call x1, Pallas kernels, on_device(): pl.pallas_call(hand_on, out_shape=tuple((jax.ShapeDtypeStruct(o.shape, o....  5.07 us

profile of v3, /device:TPU:1, one launch (start us, length us, event | category | flops | bytes accessed | tf_op | source)
XLA Modules:
  0.0 108.3 jit_solution(16839290342675135141)
XLA Ops:
  0.6 102.4 %layer.1 = (bf16[24,1024]{1,0:T(8,128)(2,1)}, bf16[24,1024]{1,0:T(8,128)(2,1)}, bf16[1024,896]{1,0:T(8,128)(2,1)}, bf16[1024,896]{1,0:T(8,128)(2,1)}, bf16[896,1024]{1,0:T(8,128)(2,1)}) custom-call(bf16[24,1024]{1,0:T(8,128)(2,1)} %refs_0_.1, bf16[1024,896]{1,0:T(8,128)(2,1)} %refs_1_.1, bf16[1024,896]{1,0:T(8,128)(2,1)} %refs_2_.1, ...), custom_call_target="tpu_custom_call" | custom-call | flops 12683575296 | bytes 12582912 | tf_op jit(solution)/shard_map/layer/pallas_call | solution.py:502
  103.1 5.1 %hand_on.1 = (bf16[24,1024]{1,0:T(8,128)(2,1)}, bf16[24,1024]{1,0:T(8,128)(2,1)}, bf16[1024,896]{1,0:T(8,128)(2,1)}, bf16[1024,896]{1,0:T(8,128)(2,1)}, bf16[896,1024]{1,0:T(8,128)(2,1)}) custom-call(bf16[24,1024]{1,0:T(8,128)(2,1)} %get-tuple-element.10.refs_0_, bf16[24,1024]{1,0:T(8,128)(2,1)} %get-tuple-element.11.refs_1_, ...), custom_call_target="tpu_custom_call" | custom-call | bytes 12582912 | tf_op jit(solution)/shard_map/hand_on/pallas_call | solution.py:520

commit v4 on v3

--- a/solution.py
+++ b/solution.py
@@ -126,12 +126,17 @@
         leaving.append(d)
 
     def got(*keys):
-        while len(leaving) > 40:
+        while len(leaving) > 20:
             leaving.pop(0).wait_send()
         for key in keys:
             if key not in waited:
                 waited.add(key)
                 sent[key].wait_recv()
+
+    barrier = pltpu.get_barrier_semaphore()
+    peers = [RIGHT, LEFT, YH, SIB, YL, ZL(1, 1), ZL(7, 1)] + [ZL(dz) for dz in range(1, 8)]
+    for to in peers:
+        pl.semaphore_signal(barrier, inc=1, device_id=to, device_id_type=MESH)
 
     loads = [
         pltpu.make_async_copy(tok_in, io_buf.at[0], lsem.at[0]),
@@ -143,11 +148,6 @@
     for d in loads:
         d.start()
     stores = []
-
-    barrier = pltpu.get_barrier_semaphore()
-    peers = [RIGHT, LEFT, YH, SIB, YL, ZL(1, 1), ZL(7, 1)] + [ZL(dz) for dz in range(1, 8)]
-    for to in peers:
-        pl.semaphore_signal(barrier, inc=1, device_id=to, device_id_type=MESH)
 
     def pack(v):
         v = v.astype(F32)

time: 108 us -> 109 us (level)
  no operation moved by 1% of the time
where the time goes in v4:
time: 109 us
  Pallas kernels  108 us (99%)
    pallas_call x1, Pallas kernels, on_device(): pl.pallas_call(kernel, out_shape=(jax.ShapeDtypeStruct((OWN, W), BF), jax...  103 us
    pallas_call x1, Pallas kernels, on_device(): pl.pallas_call(hand_on, out_shape=tuple((jax.ShapeDtypeStruct(o.shape, o....  5.07 us

profile of v4, /device:TPU:1, one launch (start us, length us, event | category | flops | bytes accessed | tf_op | source)
XLA Modules:
  0.0 108.7 jit_solution(15957733653673666403)
XLA Ops:
  0.6 102.8 %layer.1 = (bf16[24,1024]{1,0:T(8,128)(2,1)}, bf16[24,1024]{1,0:T(8,128)(2,1)}, bf16[1024,896]{1,0:T(8,128)(2,1)}, bf16[1024,896]{1,0:T(8,128)(2,1)}, bf16[896,1024]{1,0:T(8,128)(2,1)}) custom-call(bf16[24,1024]{1,0:T(8,128)(2,1)} %refs_0_.1, bf16[1024,896]{1,0:T(8,128)(2,1)} %refs_1_.1, bf16[1024,896]{1,0:T(8,128)(2,1)} %refs_2_.1, ...), custom_call_target="tpu_custom_call" | custom-call | flops 12683575296 | bytes 12582912 | tf_op jit(solution)/shard_map/layer/pallas_call | solution.py:502
  103.4 5.1 %hand_on.1 = (bf16[24,1024]{1,0:T(8,128)(2,1)}, bf16[24,1024]{1,0:T(8,128)(2,1)}, bf16[1024,896]{1,0:T(8,128)(2,1)}, bf16[1024,896]{1,0:T(8,128)(2,1)}, bf16[896,1024]{1,0:T(8,128)(2,1)}) custom-call(bf16[24,1024]{1,0:T(8,128)(2,1)} %get-tuple-element.10.refs_0_, bf16[24,1024]{1,0:T(8,128)(2,1)} %get-tuple-element.11.refs_1_, ...), custom_call_target="tpu_custom_call" | custom-call | bytes 12582912 | tf_op jit(solution)/shard_map/hand_on/pallas_call | solution.py:520
